TPU v7x, 32 devices: a whole 2x2x4 slice. The times are simulated.
32 devices in a mesh: frame: 4 (over x, core), row: 8 (over z, y).
Axes of the slice: x: 2, y: 2, z: 4, core: 2. Of those that a mesh axis runs over, the one named last changes fastest.
Arguments:
- queries: bfloat16 [4, 64, 16, 1536], P('frame', 'row'), may hold values from -128 to 128
- keys: bfloat16 [4, 64, 16, 1536], P('frame', 'row'), may hold values from -6 to 6
- values: bfloat16 [4, 64, 16, 1536], P('frame', 'row'), may hold values from -6 to 6
- window_mask: int32 [4, 8, 2, 45], P('frame', 'row'), may hold values 0 or 1
- tile_valid: int32 [4, 8, 2], replicated, may hold values 0 or 1
- w_out: bfloat16 [1536, 3072], replicated, may hold values from -0.5 to 0.5
- gate: float32 [3072], replicated, may hold values from 0.5 to 4
Outputs:
- update: bfloat16 [4, 64, 16, 3072], P('frame', 'row')
All inputs are finite; a program needn't handle non-finite values. No bound on the sum of `window_mask` on one device may be relied on, other than what follows from the above.
Results may differ from a plain program's by a relative error of at most 0.0053.
Values may be sent and summed in bfloat16 or wider, within the bound.
A program may use at most 128 MiB of HBM per device.

v0:
```python
import math

import jax
import jax.numpy as jnp
from jax import lax
from jax.sharding import PartitionSpec as P

HEADS = 12
HD = 128


def from_behind(value, axis, steps):
    count = lax.axis_size(axis)
    initial, last = (max(0, -steps), min(count, count - steps))
    return lax.ppermute(value, axis, [(source, source + steps) for source in range(initial, last)])


def padded(array, sides, width):
    for axis, dim in sides:
        devices, length = (lax.axis_size(axis), array.shape[dim])
        up = [(i, (i + 1) % devices) for i in range(devices - 1)]
        down = [(j, i) for i, j in up]
        last = lax.slice_in_dim(array, length - width, length, axis=dim)
        initial = lax.slice_in_dim(array, 0, width, axis=dim)
        before = lax.ppermute(last, axis, up)
        after = lax.ppermute(initial, axis, down)
        array = jnp.concatenate([before, array, after], axis=dim)
    return array


def tile_usage(offset_mask, tile_flags):
    col_tiles = offset_mask.shape[0]
    window_table = offset_mask.reshape(col_tiles, 3, 5, 3) == 1
    inside = tile_flags[:, :, 1 : col_tiles + 1] == 1
    query_col = jnp.arange(col_tiles)[:, None]
    key_col = jnp.arange(col_tiles)[None, :]
    centre = (jnp.arange(3)[:, None] == 1) & (jnp.arange(5)[None, :] == 2)
    usable = jnp.zeros((col_tiles, 3, 5, col_tiles), dtype=bool)
    for shift_col in (-1, 0, 1):
        col_pair = key_col - query_col == shift_col
        allowed = window_table[:, :, :, shift_col + 1][:, :, :, None] & inside[None]
        if shift_col == 0:
            allowed = allowed | centre[None, :, :, None]
        usable = usable | col_pair[:, None, None, :] & allowed
    return usable


def attend_block(queries, key_ext, value_ext, usable, w_out, gate):
    frames, rows_here, columns, width = queries.shape
    col_tiles = usable.shape[0]
    tile_w = columns // col_tiles
    tok_count = frames * rows_here * columns
    key_count = key_ext.shape[0] * key_ext.shape[1] * columns
    key_mask = jnp.broadcast_to(
        usable.reshape(1, 1, col_tiles, 1, 3, 1, 5, 1, col_tiles, 1),
        (frames, rows_here, col_tiles, tile_w, 3, frames, 5, rows_here, col_tiles, tile_w),
    ).reshape(tok_count, key_count)
    flat_query = queries.reshape(tok_count, width)
    flat_key = key_ext.reshape(key_count, width)
    flat_value = value_ext.reshape(key_count, width)
    score_scale = 1.0 / math.sqrt(HD)

    def one_head(head_id):
        start = head_id * HD
        query_head = lax.dynamic_slice_in_dim(flat_query, start, HD, 1)
        key_head = lax.dynamic_slice_in_dim(flat_key, start, HD, 1)
        value_head = lax.dynamic_slice_in_dim(flat_value, start, HD, 1)
        scores = jnp.dot(query_head, key_head.T, preferred_element_type=jnp.float32) * score_scale
        scores = jnp.where(key_mask, scores, -1e30)
        highest = jnp.max(scores, axis=1, keepdims=True)
        weights = jnp.where(key_mask, jnp.exp(scores - highest), 0.0)
        totals = jnp.sum(weights, axis=1, keepdims=True)
        mixed = jnp.dot(
            weights.astype(jnp.bfloat16), value_head, preferred_element_type=jnp.float32
        )
        return mixed / totals

    head_outs = lax.map(one_head, jnp.arange(HEADS, dtype=jnp.int32))
    attention = head_outs.transpose(1, 0, 2).reshape(tok_count, width).astype(jnp.bfloat16)
    update = jnp.dot(attention, w_out, preferred_element_type=jnp.float32) * gate[None, :]
    return update.astype(jnp.bfloat16).reshape(frames, rows_here, columns, w_out.shape[1])


def reach_far(block, offset):
    return from_behind(block, "row", offset)


def widen_rows(block):
    pieces = [
        reach_far(block, 2),
        reach_far(block, 1),
        block,
        reach_far(block, -1),
        reach_far(block, -2),
    ]
    return jnp.concatenate(pieces, axis=2)


def local(queries, keys, values, window_mask, tile_valid, w_out, gate):
    frames = queries.shape[0]
    col_tiles = window_mask.shape[2]
    paired = jnp.stack((keys, values), 0)
    extended = widen_rows(paired)
    extended = padded(extended, (("frame", 1),), frames)
    frame_idx = lax.axis_index("frame")
    row_idx = lax.axis_index("row")
    padded_flags = jnp.pad(tile_valid, ((1, 1), (2, 2), (1, 1)))
    tile_flags = lax.dynamic_slice(
        padded_flags, (frame_idx, row_idx, jnp.int32(0)), (3, 5, col_tiles + 2)
    )
    usable = tile_usage(window_mask[0, 0], tile_flags)
    return attend_block(queries, extended[0], extended[1], usable, w_out, gate)


def solution(mesh):
    placed = (
        P("frame", "row", None, None),
        P("frame", "row", None, None),
        P("frame", "row", None, None),
        P("frame", "row", None, None),
        P(),
        P(),
        P(),
    )
    return jax.shard_map(
        local, mesh=mesh, in_specs=placed, out_specs=P("frame", "row", None, None), check_vma=False
    )
```

profile of v0, /device:TPU:1, one launch (start us, length us, event | category | flops | bytes accessed | tf_op | source)
XLA Modules:
  0.0 483.3 jit_solution(2675286478773118511)
XLA Ops:
  11.2 10.3 %collective-permute-done = bf16[2,1,8,16,1536]{4,3,2,1,0:T(8,128)(2,1)S(1)} collective-permute-done((bf16[2,1,8,16,1536]{4,3,2,1,0:T(8,128)(2,1)S(1)}, bf16[2,1,8,16,1536]{4,3,2,1,0:T(8,128)(2,1)S(1)}, u32[]{:S(2)}, u32[]{:S(2)}) %collective-permute-start) | collective-permute-done | bytes 786464 | tf_op jit(solution)/shard_map/ppermute | solution.py:15
  22.5 18.8 %collective-permute-done.1 = bf16[2,1,8,16,1536]{4,3,2,1,0:T(8,128)(2,1)S(1)} collective-permute-done((bf16[2,1,8,16,1536]{4,3,2,1,0:T(8,128)(2,1)S(1)}, bf16[2,1,8,16,1536]{4,3,2,1,0:T(8,128)(2,1)S(1)}, u32[]{:S(2)}, u32[]{:S(2)}) %collective-permute-start.1) | collective-permute-done | bytes 786464 | tf_op jit(solution)/shard_map/ppermute | solution.py:15
  55.3 39.8 %collective-permute-done.4 = bf16[2,1,40,16,1536]{4,3,2,1,0:T(8,128)(2,1)} collective-permute-done((bf16[2,1,40,16,1536]{4,3,2,1,0:T(8,128)(2,1)}, bf16[2,1,40,16,1536]{4,3,2,1,0:T(8,128)(2,1)}, u32[]{:S(2)}, u32[]{:S(2)}) %collective-permute-start.4) | collective-permute-done | bytes 3932192 | tf_op jit(solution)/shard_map/ppermute | solution.py:25
  110.3 367.1 %while.11 = (s32[]{:T(128)}, bf16[12,128,128]{1,2,0:T(8,128)(2,1)S(1)}, s32[12]{0:T(128)S(1)}, bf16[128,1536]{1,0:T(8,128)(2,1)}, bf16[1920,1536]{1,0:T(8,128)(2...) while((s32[]{:T(128)}, ...), condition=%wide.region_3.4_spmd.clone, body=%wide.region_0.3_spmd.clone.sunk | while | flops 128073472 | bytes 5607147 | solution.py:78
  111.5 6.4 %broadcast_in_dim.61 = pred[8,2,8,3,1,5,8,2,8]{8,7,6,5,3,2,1,0,4:T(4,128)(4,1)} broadcast(pred[2,3,5,2]{3,2,1,0:T(8,128)(4,1)S(1)} %get-tuple-element.158), dimensions={1,3,5,7} | broadcast | bytes 245820 | tf_op jit(solution)/shard_map/broadcast_in_dim | solution.py:54
  117.9 19.5 %broadcast_in_dim.62 = pred[128,1920]{1,0:T(32,128)(4,1)S(1)} reshape(pred[8,2,8,3,1,5,8,2,8]{8,7,6,5,3,2,1,0,4:T(4,128)(4,1)} %broadcast_in_dim.61) | data formatting | bytes 491520 | tf_op jit(solution)/shard_map/broadcast_in_dim | solution.py:54
  142.1 6.4 %broadcast_in_dim.61 = pred[8,2,8,3,1,5,8,2,8]{8,7,6,5,3,2,1,0,4:T(4,128)(4,1)} broadcast(pred[2,3,5,2]{3,2,1,0:T(8,128)(4,1)S(1)} %get-tuple-element.158), dimensions={1,3,5,7} | broadcast | bytes 245820 | tf_op jit(solution)/shard_map/broadcast_in_dim | solution.py:54
  148.5 19.5 %broadcast_in_dim.62 = pred[128,1920]{1,0:T(32,128)(4,1)S(1)} reshape(pred[8,2,8,3,1,5,8,2,8]{8,7,6,5,3,2,1,0,4:T(4,128)(4,1)} %broadcast_in_dim.61) | data formatting | bytes 491520 | tf_op jit(solution)/shard_map/broadcast_in_dim | solution.py:54
  172.7 6.4 %broadcast_in_dim.61 = pred[8,2,8,3,1,5,8,2,8]{8,7,6,5,3,2,1,0,4:T(4,128)(4,1)} broadcast(pred[2,3,5,2]{3,2,1,0:T(8,128)(4,1)S(1)} %get-tuple-element.158), dimensions={1,3,5,7} | broadcast | bytes 245820 | tf_op jit(solution)/shard_map/broadcast_in_dim | solution.py:54
  179.1 19.5 %broadcast_in_dim.62 = pred[128,1920]{1,0:T(32,128)(4,1)S(1)} reshape(pred[8,2,8,3,1,5,8,2,8]{8,7,6,5,3,2,1,0,4:T(4,128)(4,1)} %broadcast_in_dim.61) | data formatting | bytes 491520 | tf_op jit(solution)/shard_map/broadcast_in_dim | solution.py:54
  203.3 6.4 %broadcast_in_dim.61 = pred[8,2,8,3,1,5,8,2,8]{8,7,6,5,3,2,1,0,4:T(4,128)(4,1)} broadcast(pred[2,3,5,2]{3,2,1,0:T(8,128)(4,1)S(1)} %get-tuple-element.158), dimensions={1,3,5,7} | broadcast | bytes 245820 | tf_op jit(solution)/shard_map/broadcast_in_dim | solution.py:54
  209.7 19.5 %broadcast_in_dim.62 = pred[128,1920]{1,0:T(32,128)(4,1)S(1)} reshape(pred[8,2,8,3,1,5,8,2,8]{8,7,6,5,3,2,1,0,4:T(4,128)(4,1)} %broadcast_in_dim.61) | data formatting | bytes 491520 | tf_op jit(solution)/shard_map/broadcast_in_dim | solution.py:54
  233.9 6.4 %broadcast_in_dim.61 = pred[8,2,8,3,1,5,8,2,8]{8,7,6,5,3,2,1,0,4:T(4,128)(4,1)} broadcast(pred[2,3,5,2]{3,2,1,0:T(8,128)(4,1)S(1)} %get-tuple-element.158), dimensions={1,3,5,7} | broadcast | bytes 245820 | tf_op jit(solution)/shard_map/broadcast_in_dim | solution.py:54
  240.3 19.5 %broadcast_in_dim.62 = pred[128,1920]{1,0:T(32,128)(4,1)S(1)} reshape(pred[8,2,8,3,1,5,8,2,8]{8,7,6,5,3,2,1,0,4:T(4,128)(4,1)} %broadcast_in_dim.61) | data formatting | bytes 491520 | tf_op jit(solution)/shard_map/broadcast_in_dim | solution.py:54
  264.5 6.4 %broadcast_in_dim.61 = pred[8,2,8,3,1,5,8,2,8]{8,7,6,5,3,2,1,0,4:T(4,128)(4,1)} broadcast(pred[2,3,5,2]{3,2,1,0:T(8,128)(4,1)S(1)} %get-tuple-element.158), dimensions={1,3,5,7} | broadcast | bytes 245820 | tf_op jit(solution)/shard_map/broadcast_in_dim | solution.py:54
  270.8 19.5 %broadcast_in_dim.62 = pred[128,1920]{1,0:T(32,128)(4,1)S(1)} reshape(pred[8,2,8,3,1,5,8,2,8]{8,7,6,5,3,2,1,0,4:T(4,128)(4,1)} %broadcast_in_dim.61) | data formatting | bytes 491520 | tf_op jit(solution)/shard_map/broadcast_in_dim | solution.py:54
  301.4 19.5 %broadcast_in_dim.62 = pred[128,1920]{1,0:T(32,128)(4,1)S(1)} reshape(pred[8,2,8,3,1,5,8,2,8]{8,7,6,5,3,2,1,0,4:T(4,128)(4,1)} %broadcast_in_dim.61) | data formatting | bytes 491520 | tf_op jit(solution)/shard_map/broadcast_in_dim | solution.py:54
  332.0 19.5 %broadcast_in_dim.62 = pred[128,1920]{1,0:T(32,128)(4,1)S(1)} reshape(pred[8,2,8,3,1,5,8,2,8]{8,7,6,5,3,2,1,0,4:T(4,128)(4,1)} %broadcast_in_dim.61) | data formatting | bytes 491520 | tf_op jit(solution)/shard_map/broadcast_in_dim | solution.py:54
  362.6 19.5 %broadcast_in_dim.62 = pred[128,1920]{1,0:T(32,128)(4,1)S(1)} reshape(pred[8,2,8,3,1,5,8,2,8]{8,7,6,5,3,2,1,0,4:T(4,128)(4,1)} %broadcast_in_dim.61) | data formatting | bytes 491520 | tf_op jit(solution)/shard_map/broadcast_in_dim | solution.py:54
  386.8 6.4 %broadcast_in_dim.61 = pred[8,2,8,3,1,5,8,2,8]{8,7,6,5,3,2,1,0,4:T(4,128)(4,1)} broadcast(pred[2,3,5,2]{3,2,1,0:T(8,128)(4,1)S(1)} %get-tuple-element.158), dimensions={1,3,5,7} | broadcast | bytes 245820 | tf_op jit(solution)/shard_map/broadcast_in_dim | solution.py:54
  393.2 19.5 %broadcast_in_dim.62 = pred[128,1920]{1,0:T(32,128)(4,1)S(1)} reshape(pred[8,2,8,3,1,5,8,2,8]{8,7,6,5,3,2,1,0,4:T(4,128)(4,1)} %broadcast_in_dim.61) | data formatting | bytes 491520 | tf_op jit(solution)/shard_map/broadcast_in_dim | solution.py:54
  417.4 6.4 %broadcast_in_dim.61 = pred[8,2,8,3,1,5,8,2,8]{8,7,6,5,3,2,1,0,4:T(4,128)(4,1)} broadcast(pred[2,3,5,2]{3,2,1,0:T(8,128)(4,1)S(1)} %get-tuple-element.158), dimensions={1,3,5,7} | broadcast | bytes 245820 | tf_op jit(solution)/shard_map/broadcast_in_dim | solution.py:54
  423.8 19.5 %broadcast_in_dim.62 = pred[128,1920]{1,0:T(32,128)(4,1)S(1)} reshape(pred[8,2,8,3,1,5,8,2,8]{8,7,6,5,3,2,1,0,4:T(4,128)(4,1)} %broadcast_in_dim.61) | data formatting | bytes 491520 | tf_op jit(solution)/shard_map/broadcast_in_dim | solution.py:54
  454.4 19.5 %broadcast_in_dim.62 = pred[128,1920]{1,0:T(32,128)(4,1)S(1)} reshape(pred[8,2,8,3,1,5,8,2,8]{8,7,6,5,3,2,1,0,4:T(4,128)(4,1)} %broadcast_in_dim.61) | data formatting | bytes 491520 | tf_op jit(solution)/shard_map/broadcast_in_dim | solution.py:54
  (117 shorter events, 120.7 us)
Async XLA Ops:
  0.0 42.2 %copy-start.1 = (bf16[1,8,16,1536]{3,2,1,0:T(8,128)(2,1)S(1)}, bf16[1,8,16,1536]{3,2,1,0:T(8,128)(2,1)}, u32[]{:S(2)}) copy-start(bf16[1,8,16,1536]{3,2,1,0:T(8,128)(2,1)} %param.10) | copy-start | bytes 1179652
  0.0 42.2 %copy-start = (bf16[1,8,16,1536]{3,2,1,0:T(8,128)(2,1)S(1)}, bf16[1,8,16,1536]{3,2,1,0:T(8,128)(2,1)}, u32[]{:S(2)}) copy-start(bf16[1,8,16,1536]{3,2,1,0:T(8,128)(2,1)} %param.11) | copy-start | bytes 1179652
  1.3 53.0 %copy-start.3 = (s32[4,8,2]{1,2,0:T(2,128)S(1)}, s32[4,8,2]{1,2,0:T(2,128)}, u32[]{:S(2)}) copy-start(s32[4,8,2]{1,2,0:T(2,128)} %param.13) | copy-start | bytes 772
  1.3 53.2 %copy-start.4 = (s32[1,1,2,45]{3,2,1,0:T(2,128)S(1)}, s32[1,1,2,45]{3,2,1,0:T(2,128)}, u32[]{:S(2)}) copy-start(s32[1,1,2,45]{3,2,1,0:T(2,128)} %param.12) | copy-start | bytes 1084
  1.3 20.2 %collective-permute-start = (bf16[2,1,8,16,1536]{4,3,2,1,0:T(8,128)(2,1)S(1)}, bf16[2,1,8,16,1536]{4,3,2,1,0:T(8,128)(2,1)S(1)}, u32[]{:S(2)}, u32[]{:S(2)}) collective-permute-start(bf16[2,1,8,16,1536]{4,3,2,1,0:T(8,128)(2,1)S(1)} %pad_maximum_fusion.1), channel_id=1, source_target_pairs={{0,2},{1,3},{2,4},{3,5},{4,6},{5,7},{8,10},{9,11},{10,12},{11,13},... | collective-permute-start | bytes 2359304 | tf_op jit(solution)/shard_map/ppermute | solution.py:15
  5.4 35.9 %collective-permute-start.1 = (bf16[2,1,8,16,1536]{4,3,2,1,0:T(8,128)(2,1)S(1)}, bf16[2,1,8,16,1536]{4,3,2,1,0:T(8,128)(2,1)S(1)}, u32[]{:S(2)}, u32[]{:S(2)}) collective-permute-start(bf16[2,1,8,16,1536]{4,3,2,1,0:T(8,128)(2,1)S(1)} %pad_maximum_fusion.1), channel_id=1, source_target_pairs={{0,1},{1,2},{2,3},{3,4},{4,5},{5,6},{6,7},{8,9},{9,10},{10,11},{11... | collective-permute-start | bytes 2359304 | tf_op jit(solution)/shard_map/ppermute | solution.py:15
  8.6 34.6 %collective-permute-start.2 = (bf16[2,1,8,16,1536]{4,3,2,1,0:T(8,128)(2,1)S(1)}, bf16[2,1,8,16,1536]{4,3,2,1,0:T(8,128)(2,1)S(1)}, u32[]{:S(2)}, u32[]{:S(2)}) collective-permute-start(bf16[2,1,8,16,1536]{4,3,2,1,0:T(8,128)(2,1)S(1)} %pad_maximum_fusion.1), channel_id=1, source_target_pairs={{1,0},{2,1},{3,2},{4,3},{5,4},{6,5},{7,6},{9,8},{10,9},{11,10},{12... | collective-permute-start | bytes 2359304 | tf_op jit(solution)/shard_map/ppermute | solution.py:15
  9.9 36.2 %collective-permute-start.3 = (bf16[2,1,8,16,1536]{4,3,2,1,0:T(8,128)(2,1)S(1)}, bf16[2,1,8,16,1536]{4,3,2,1,0:T(8,128)(2,1)S(1)}, u32[]{:S(2)}, u32[]{:S(2)}) collective-permute-start(bf16[2,1,8,16,1536]{4,3,2,1,0:T(8,128)(2,1)S(1)} %pad_maximum_fusion.1), channel_id=1, source_target_pairs={{2,0},{3,1},{4,2},{5,3},{6,4},{7,5},{10,8},{11,9},{12,10},{13,11},... | collective-permute-start | bytes 2359304 | tf_op jit(solution)/shard_map/ppermute | solution.py:15
  47.0 48.0 %collective-permute-start.4 = (bf16[2,1,40,16,1536]{4,3,2,1,0:T(8,128)(2,1)}, bf16[2,1,40,16,1536]{4,3,2,1,0:T(8,128)(2,1)}, u32[]{:S(2)}, u32[]{:S(2)}) collective-permute-start(bf16[2,1,40,16,1536]{4,3,2,1,0:T(8,128)(2,1)} %constant_dynamic-update-slice_fusion.1), channel_id=1, source_target_pairs={{0,8},{8,16},{16,24},{1,9},{9,17},{17,25},{2,10},{10,18},{18,26},{... | collective-permute-start | bytes 11796488 | tf_op jit(solution)/shard_map/ppermute | solution.py:25
  52.1 47.3 %collective-permute-start.5 = (bf16[2,1,40,16,1536]{4,3,2,1,0:T(8,128)(2,1)}, bf16[2,1,40,16,1536]{4,3,2,1,0:T(8,128)(2,1)}, u32[]{:S(2)}, u32[]{:S(2)}) collective-permute-start(bf16[2,1,40,16,1536]{4,3,2,1,0:T(8,128)(2,1)} %constant_dynamic-update-slice_fusion.1), channel_id=1, source_target_pairs={{8,0},{16,8},{24,16},{9,1},{17,9},{25,17},{10,2},{18,10},{26,18},{... | collective-permute-start | bytes 11796488 | tf_op jit(solution)/shard_map/ppermute | solution.py:26
  110.3 367.1 %copy-start.2 = (f32[3072]{0:T(1024)S(1)}, f32[3072]{0:T(1024)}, u32[]{:S(2)}) copy-start(f32[3072]{0:T(1024)} %param.15) | copy-start | bytes 36868
where the time goes:
time: 485 us; the launch traced here: 483 us
  local copies, waits for them, and re-layouts  329 us (68%)
  waiting for transfers between devices  75.2 us (16%)
  matrix products  40.6 us (8%)
  starting transfers between devices  17.1 us (4%)
  other arithmetic  13.1 us (3%)
  loops' own time  8.23 us (2%)
    broadcast_in_dim x24, local copies, waits for them, and re-layouts, attend_block(): jnp.broadcast_to(usable.reshape(1, 1, col_tiles, 1, 3, 1, 5, 1, col_tiles...  311 us
    ppermute x1, waiting for transfers between devices, padded(): before = lax.ppermute(last, axis, up)  39.8 us
    ppermute x4, waiting for transfers between devices, from_behind(): lax.ppermute(value, axis, [(source, source + steps) for source in range(i...  31 us
    dot_general x12, matrix products, one_head(): jnp.dot(query_head, key_head.T, preferred_element_type=jnp.float32)  17.4 us
    dot_general x12, matrix products, one_head(): jnp.dot(weights.astype(jnp.bfloat16), value_head, preferred_element_type=...  17.1 us
    ppermute x4, starting transfers between devices, from_behind(): lax.ppermute(value, axis, [(source, source + steps) for source in range(i...  9.86 us
  transfers between devices with their start and end apart: 6, of which 5 were waited for; matrix products, arithmetic and copies ran while one was open for 1% of the time, Pallas kernels for 0%

commit v1 on v0

v1 whole, which is shorter than its diff:
```python
import functools
import math

import jax
import jax.numpy as jnp
from jax import lax
from jax.experimental import pallas as pl
from jax.experimental.pallas import tpu as pltpu
from jax.sharding import PartitionSpec as P

HD = 128
FLOOR = -1e20
BLOCKED = -1e30
MESH = pl.DeviceIdType.MESH
GROUPS = 4


def kernel(
    nf, nr, groups,
    q_hbm, k_hbm, v_hbm, wm, tv, w_hbm, gate_ref, out_ref,
    k3, v3, vt, qb, bias_own, bias_in, bias_y, o_out, o_in, own, lse_own,
    y_out, y_in, w_v, acc,
    kv_s, kv_r, qy_s, qy_r, qf_s, qf_r, of_s, of_r, oy_s, oy_r,
    by_s, by_r, bf_s, bf_r, loc, wloc,
):
    tok = q_hbm.shape[0]
    width = q_hbm.shape[1]
    gw = width // groups
    gh = gw // HD
    col_tiles = wm.shape[2]
    f = lax.axis_index("frame")
    r = lax.axis_index("row")
    y = r % 2
    ry = r + 1 - 2 * y
    f_has = (f < nf - 1, f > 0)
    f_dev = ((f + 1, r), (f - 1, r))
    r_has = (r + 2 < nr, r >= 2)
    r_dev = ((f, r + 2), (f, r - 2))
    land = (tok * (2 - y), tok * (1 + y))
    came = (1, 0)
    scale = math.log2(math.e) / math.sqrt(HD)

    barrier = pltpu.get_barrier_semaphore()
    pl.semaphore_signal(barrier, inc=1, device_id=(f, ry), device_id_type=MESH)
    for has, dev in zip(f_has + r_has, f_dev + r_dev):
        @pl.when(has)
        def _(dev=dev):
            pl.semaphore_signal(barrier, inc=1, device_id=dev, device_id_type=MESH)

    locals_ = [
        pltpu.make_async_copy(q_hbm, qb.at[0, 1], loc.at[0]),
        pltpu.make_async_copy(k_hbm, k3.at[pl.ds(0, tok)], loc.at[1]),
        pltpu.make_async_copy(v_hbm, v3.at[pl.ds(0, tok)], loc.at[2]),
    ]
    for c in locals_:
        c.start()

    def cols(g):
        return pl.ds(pl.multiple_of(g * gw, gw), gw)

    def remote(src, dst, s, d, dev):
        return pltpu.make_async_remote_copy(
            src_ref=src, dst_ref=dst, send_sem=s, recv_sem=d,
            device_id=dev, device_id_type=MESH)

    def kv_copy(way, which, g):
        src = (k_hbm, v_hbm)[which]
        dst = (k3, v3)[which]
        rows = pl.ds(pl.multiple_of(land[way], tok), tok)
        return remote(src.at[:, cols(g)], dst.at[rows, cols(g)],
                      kv_s.at[way, which, g], kv_r.at[way, which, g], r_dev[way])

    def qy_copy(g):
        return remote(q_hbm.at[:, cols(g)], qb.at[1, 1, :, cols(g)],
                      qy_s.at[g], qy_r.at[g], (f, ry))

    def qf_copy(way, p, g):
        src = q_hbm.at[:, cols(g)] if p == 0 else qb.at[1, 1, :, cols(g)]
        return remote(src, qb.at[p, 2 * way, :, cols(g)],
                      qf_s.at[way, p, g], qf_r.at[way, p, g], f_dev[way])

    def of_copy(way, p, g):
        return remote(o_out.at[way, p, g], o_in.at[way, p, g],
                      of_s.at[way, p, g], of_r.at[way, p, g], f_dev[way])

    def oy_copy(g):
        return remote(y_out.at[g], y_in.at[g], oy_s.at[g], oy_r.at[g], (f, ry))

    def by_copy():
        return remote(bias_own.at[1], bias_y, by_s, by_r, (f, ry))

    def bf_copy(way, p):
        at = 2 - 2 * way
        src = bias_own.at[0, at] if p == 0 else bias_y.at[at]
        return remote(src, bias_in.at[p, way], bf_s.at[way, p], bf_r.at[way, p], f_dev[way])

    lane_col = (lax.broadcasted_iota(jnp.int32, (1, tok), 1) // 8) % col_tiles
    row8 = lax.broadcasted_iota(jnp.int32, (8, tok), 0)
    row_of = (
        (2, 4 - 4 * y, 4 * y),
        (3 - 2 * y, 1 + 2 * y),
    )
    for p in range(2):
        for df in range(3):
            block = jnp.zeros((8, tok), jnp.float32)
            for slot, dr in enumerate(row_of[p]):
                kf = f + df - 1
                kr = r + dr - 2
                inside = jnp.logical_and(
                    jnp.logical_and(kf >= 0, kf < nf), jnp.logical_and(kr >= 0, kr < nr))
                kfc = jnp.clip(kf, 0, nf - 1)
                krc = jnp.clip(kr, 0, nr - 1)
                for kc in range(col_tiles):
                    valid = jnp.where(inside, tv[kfc, krc, kc], 0)
                    line = jnp.full((1, tok), BLOCKED, jnp.float32)
                    for qc in range(col_tiles):
                        ds = kc - qc
                        if abs(ds) > 1:
                            continue
                        if p == 0 and df == 1 and slot == 0 and ds == 0:
                            val = jnp.float32(0.0)
                        else:
                            o = 15 * df + 3 * dr + ds + 1
                            ok = jnp.where(wm[0, 0, qc, o] == 1, valid, 0)
                            val = jnp.where(ok == 1, 0.0, BLOCKED).astype(jnp.float32)
                        line = jnp.where(lane_col == qc, val, line)
                    block = jnp.where(row8 == slot * col_tiles + kc, line, block)
            bias_own[p, df] = block

    for way in range(2):
        @pl.when(jnp.logical_not(r_has[came[way]]))
        def _(way=way):
            rows = pl.ds(pl.multiple_of(land[way], tok), tok)
            k3[rows, :] = jnp.zeros((tok, width), k3.dtype)
            v3[rows, :] = jnp.zeros((tok, width), v3.dtype)

        @pl.when(jnp.logical_not(f_has[came[way]]))
        def _(way=way):
            lines = o_in.shape[3]
            first = lax.broadcasted_iota(jnp.int32, (lines, tok), 0)
            fill = jnp.where(
                jnp.logical_and(first >= gw, first < gw + gh), FLOOR, 0.0).astype(o_in.dtype)
            for p in range(2):
                for g in range(groups):
                    o_in[way, p, g] = fill

    count = 1 + sum(h.astype(jnp.int32) for h in f_has + r_has)
    pl.semaphore_wait(barrier, count)

    by_copy().start()
    for way in range(2):
        @pl.when(f_has[way])
        def _(way=way):
            bf_copy(way, 0).start()

    @pl.loop(0, groups)
    def _(g):
        qy_copy(g).start()
        for way in range(2):
            @pl.when(f_has[way])
            def _(way=way):
                qf_copy(way, 0, g).start()

            @pl.when(r_has[way])
            def _(way=way):
                kv_copy(way, 0, g).start()
                kv_copy(way, 1, g).start()

    w_copy = pltpu.make_async_copy(w_hbm, w_v, wloc)
    w_copy.start()

    by_copy().wait_recv()
    for way in range(2):
        @pl.when(f_has[way])
        def _(way=way):
            bf_copy(way, 1).start()

        @pl.when(f_has[came[way]])
        def _(way=way):
            bf_copy(way, 0).wait_recv()

    def pass_on(g):
        qy_copy(g).wait_recv()
        for way in range(2):
            @pl.when(f_has[way])
            def _(way=way):
                qf_copy(way, 1, g).start()

    pass_on(0)
    for c in locals_:
        c.wait()
    for way in range(2):
        @pl.when(f_has[came[way]])
        def _(way=way):
            bf_copy(way, 1).wait_recv()

    slots = k3.shape[0] // tok

    def attend(p, d, h, g, bias):
        n_slot = slots - p
        n = n_slot * tok
        at = pl.ds(pl.multiple_of(g * gw + h * HD, HD), HD)
        s = lax.dot_general(
            k3[pl.ds(0, n), at], qb[p, d, :, at], (((1,), (1,)), ((), ())),
            preferred_element_type=jnp.float32)
        s = s * scale
        s = s.reshape(n_slot, tok // (8 * col_tiles), col_tiles, 8, tok)
        s = s + bias[: n_slot * col_tiles].reshape(n_slot, 1, col_tiles, 1, tok)
        s = s.reshape(n, tok)
        m = jnp.maximum(jnp.max(s, axis=0, keepdims=True), FLOOR)
        e = jnp.exp2(s - m)
        total = jnp.sum(e, axis=0, keepdims=True)
        o = jnp.dot(vt[h, :, pl.ds(0, n)], e.astype(jnp.bfloat16),
                    preferred_element_type=jnp.float32)
        some = total > 0.0
        safe = jnp.where(some, total, 1.0)
        o = o * (1.0 / safe)
        lse = jnp.where(some, m + jnp.log2(safe), FLOOR)
        return o, lse

    lines = o_in.shape[3] - gw
    line_at = lax.broadcasted_iota(jnp.int32, (lines, tok), 0)

    def pack(lses):
        block = jnp.zeros((lines, tok), jnp.float32)
        for h, lse in enumerate(lses):
            rest = lse
            for j in range(3):
                piece = rest.astype(jnp.bfloat16).astype(jnp.float32)
                block = jnp.where(line_at == j * gh + h, piece, block)
                rest = rest - piece
        return block.astype(jnp.bfloat16)

    def unpack(block):
        b = block.astype(jnp.float32)
        return [b[h:h + 1] + b[gh + h:gh + h + 1] + b[2 * gh + h:2 * gh + h + 1]
                for h in range(gh)]

    def step_attend(g):
        for way in range(2):
            @pl.when(r_has[came[way]])
            def _(way=way):
                kv_copy(way, 0, g).wait_recv()
                kv_copy(way, 1, g).wait_recv()

        for h in range(gh):
            at = pl.ds(pl.multiple_of(g * gw + h * HD, HD), HD)
            vt[h] = v3[:, at].T

        for way in range(2):
            @pl.when(f_has[way])
            def _(way=way):
                d = 2 * came[way]
                for p in range(2):
                    qf_copy(came[way], p, g).wait_recv()
                for p in range(2):
                    bias = bias_in[p, came[way]]
                    lses = []
                    for h in range(gh):
                        o, lse = attend(p, d, h, g, bias)
                        o_out[way, p, g, pl.ds(h * HD, HD), :] = o.astype(jnp.bfloat16)
                        lses.append(lse)
                    o_out[way, p, g, pl.ds(gw, lines), :] = pack(lses)
                    of_copy(way, p, g).start()

        for p in range(2):
            bias = bias_own[0, 1] if p == 0 else bias_y[1]
            for h in range(gh):
                o, lse = attend(p, 1, h, g, bias)
                own[p, g, pl.ds(h * HD, HD), :] = o
                lse_own[p, g, pl.ds(h, 1), :] = lse

    def step_merge(g):
        for way in range(2):
            @pl.when(f_has[came[way]])
            def _(way=way):
                for p in range(2):
                    of_copy(way, p, g).wait_recv()
        for p in (1, 0):
            s0 = unpack(o_in[0, p, g, pl.ds(gw, lines), :])
            s1 = unpack(o_in[1, p, g, pl.ds(gw, lines), :])
            lses = []
            for h in range(gh):
                at = pl.ds(h * HD, HD)
                lo = lse_own[p, g, pl.ds(h, 1), :]
                top = jnp.maximum(jnp.maximum(s0[h], s1[h]), lo)
                w0, w1, wo = jnp.exp2(s0[h] - top), jnp.exp2(s1[h] - top), jnp.exp2(lo - top)
                z = w0 + w1 + wo
                inv = 1.0 / z
                o = (o_in[0, p, g, at, :].astype(jnp.float32) * (w0 * inv)
                     + o_in[1, p, g, at, :].astype(jnp.float32) * (w1 * inv)
                     + own[p, g, at, :] * (wo * inv))
                lse = top + jnp.log2(z)
                if p == 1:
                    y_out[g, at, :] = o.astype(jnp.bfloat16)
                    lses.append(lse)
                else:
                    own[0, g, at, :] = o
                    lse_own[0, g, pl.ds(h, 1), :] = lse
            if p == 1:
                y_out[g, pl.ds(gw, lines), :] = pack(lses)
                oy_copy(g).start()

    def step_project(g):
        oy_copy(g).wait_recv()
        s0 = unpack(y_in[g, pl.ds(gw, lines), :])
        parts = []
        for h in range(gh):
            at = pl.ds(h * HD, HD)
            lo = lse_own[0, g, pl.ds(h, 1), :]
            top = jnp.maximum(s0[h], lo)
            w0, wo = jnp.exp2(s0[h] - top), jnp.exp2(lo - top)
            inv = 1.0 / (w0 + wo)
            o = y_in[g, at, :].astype(jnp.float32) * (w0 * inv) + own[0, g, at, :] * (wo * inv)
            parts.append(o.T.astype(jnp.bfloat16))
        att = jnp.concatenate(parts, axis=1)

        @pl.when(g == 0)
        def _():
            w_copy.wait()

        rows = pl.ds(pl.multiple_of(g * gw, gw), gw)
        out_w = acc.shape[1]
        tile = 512 if out_w % 512 == 0 else out_w
        for c in range(out_w // tile):
            at = pl.ds(c * tile, tile)
            part = jnp.dot(att, w_v[rows, at], preferred_element_type=jnp.float32)

            @pl.when(g == 0)
            def _(part=part, at=at):
                acc[:, at] = part

            @pl.when(jnp.logical_and(g > 0, g < groups - 1))
            def _(part=part, at=at):
                acc[:, at] += part

            @pl.when(g == groups - 1)
            def _(part=part, at=at):
                out_ref[:, at] = ((acc[:, at] + part) * gate_ref[:, at]).astype(out_ref.dtype)

    @pl.loop(0, groups + 2)
    def _(i):
        @pl.when(i + 1 < groups)
        def _():
            pass_on(i + 1)

        @pl.when(i < groups)
        def _():
            step_attend(i)

        @pl.when(jnp.logical_and(i >= 1, i < groups + 1))
        def _():
            step_merge(i - 1)

        @pl.when(i >= 2)
        def _():
            step_project(i - 2)

    by_copy().wait_send()
    for way in range(2):
        @pl.when(f_has[way])
        def _(way=way):
            for p in range(2):
                bf_copy(way, p).wait_send()

    @pl.loop(0, groups)
    def _(g):
        qy_copy(g).wait_send()
        oy_copy(g).wait_send()
        for way in range(2):
            @pl.when(f_has[way])
            def _(way=way):
                for p in range(2):
                    qf_copy(way, p, g).wait_send()
                    of_copy(way, p, g).wait_send()

            @pl.when(r_has[way])
            def _(way=way):
                for which in range(2):
                    kv_copy(way, which, g).wait_send()


def local(nf, nr, queries, keys, values, window_mask, tile_valid, w_out, gate):
    frames, rows, columns, width = queries.shape
    tok = frames * rows * columns
    out_w = w_out.shape[1]
    heads = width // HD
    groups = GROUPS if heads % GROUPS == 0 else 1
    gw = width // groups
    gh = heads // groups
    lines = gw + 16 * (-(-3 * gh // 16))
    bf, f32 = jnp.bfloat16, jnp.float32
    hbm = pl.BlockSpec(memory_space=pl.ANY)
    smem = pl.BlockSpec(memory_space=pltpu.SMEM)
    vmem = pl.BlockSpec(memory_space=pltpu.VMEM)
    dma = pltpu.SemaphoreType.DMA
    out = pl.pallas_call(
        functools.partial(kernel, nf, nr, groups),
        out_shape=jax.ShapeDtypeStruct((tok, out_w), bf),
        in_specs=[hbm, hbm, hbm, smem, smem, hbm, vmem],
        out_specs=vmem,
        scratch_shapes=[
            pltpu.VMEM((3 * tok, width), bf),
            pltpu.VMEM((3 * tok, width), bf),
            pltpu.VMEM((gh, HD, 3 * tok), bf),
            pltpu.VMEM((2, 3, tok, width), bf),
            pltpu.VMEM((2, 3, 8, tok), f32),
            pltpu.VMEM((2, 2, 8, tok), f32),
            pltpu.VMEM((3, 8, tok), f32),
            pltpu.VMEM((2, 2, groups, lines, tok), bf),
            pltpu.VMEM((2, 2, groups, lines, tok), bf),
            pltpu.VMEM((2, groups, gw, tok), f32),
            pltpu.VMEM((2, groups, 8 * (-(-gh // 8)), tok), f32),
            pltpu.VMEM((groups, lines, tok), bf),
            pltpu.VMEM((groups, lines, tok), bf),
            pltpu.VMEM(w_out.shape, bf),
            pltpu.VMEM((tok, out_w), f32),
            dma((2, 2, groups)), dma((2, 2, groups)),
            dma((groups,)), dma((groups,)),
            dma((2, 2, groups)), dma((2, 2, groups)),
            dma((2, 2, groups)), dma((2, 2, groups)),
            dma((groups,)), dma((groups,)),
            dma, dma,
            dma((2, 2)), dma((2, 2)),
            dma((3,)), dma,
        ],
        compiler_params=pltpu.CompilerParams(
            collective_id=0, has_side_effects=True, vmem_limit_bytes=48 * 1024 * 1024),
    )(
        queries.reshape(tok, width), keys.reshape(tok, width), values.reshape(tok, width),
        window_mask, tile_valid, w_out, gate.reshape(1, out_w),
    )
    return out.reshape(frames, rows, columns, out_w)


def solution(mesh):
    split = P("frame", "row", None, None)
    nf, nr = mesh.shape["frame"], mesh.shape["row"]
    return jax.shard_map(
        functools.partial(local, nf, nr), mesh=mesh,
        in_specs=(split, split, split, split, P(), P(), P()), out_specs=split, check_vma=False,
    )
```

time: 485 us -> 44.1 us (0.09)
  local copies, waits for them, and re-layouts: 329 us -> 6.03 us
  waiting for transfers between devices: 75.2 us -> 0 us
  matrix products: 40.6 us -> 0 us
  Pallas kernels: 0 us -> 37.7 us
  starting transfers between devices: 17.1 us -> 0 us
  other arithmetic: 13.1 us -> 0 us
  loops' own time: 8.23 us -> 0 us
    broadcast_in_dim x24 -> x0, local copies, waits for them, and re-layouts: 311 us -> none  [attend_block(): jnp.broadcast_to(usable.reshape(1, 1, col_tiles, 1, 3, 1, 5, 1, col_tiles...]
    ppermute x6 -> x0, waiting for transfers between devices: 75.2 us -> none  [the longest x1 39.8 us: padded(): before = lax.ppermute(last, axis, up)]
    dot_general x25 -> x0, matrix products: 40.6 us -> none  [the longest x12 17.4 us: one_head(): jnp.dot(query_head, key_head.T, preferred_element_type=jnp.float32)]
    pallas_call x0 -> x1, Pallas kernels: none -> 37.7 us  [local(): pl.pallas_call(functools.partial(kernel, nf, nr, groups), out_shape=jax.S...]
    ppermute x6 -> x0, starting transfers between devices: 17.1 us -> none  [the longest x4 9.86 us: from_behind(): lax.ppermute(value, axis, [(source, source + steps) for source in range(i...]
    another operation x1 -> x0, loops' own time: 8.23 us -> none  [attend_block(): head_outs = lax.map(one_head, jnp.arange(HEADS, dtype=jnp.int32))]
    dynamic_slice x12 -> x0, local copies, waits for them, and re-layouts: 7.35 us -> none  [attend_block(): head_outs = lax.map(one_head, jnp.arange(HEADS, dtype=jnp.int32))]
    concatenate x1 -> x0, other arithmetic: 6.01 us -> none  [padded(): array = jnp.concatenate([before, array, after], axis=dim)]
  transfers between devices with their start and end apart: 6 -> 0, of which waited for: 5 -> 0; matrix products, arithmetic and copies ran while one was open for 1% -> 0% of each run, Pallas kernels for 0% -> 0%
where the time goes in v1:
time: 44.1 us; the launch traced here: 43.8 us
  Pallas kernels  37.7 us (85%)
  local copies, waits for them, and re-layouts  6.03 us (14%)
    pallas_call x1, Pallas kernels, local(): pl.pallas_call(functools.partial(kernel, nf, nr, groups), out_shape=jax.S...  37.7 us
    unnamed x12, local copies, waits for them, and re-layouts  6.03 us

profile of v1, /device:TPU:1, one launch (start us, length us, event | category | flops | bytes accessed | tf_op | source)
XLA Modules:
  0.0 43.8 jit_solution(781877264513394453)
XLA Ops:
  0.0 0.8 %copy.8.tv = s32[4,8,2]{2,1,0:T(8,128)S(1)} copy(s32[4,8,2]{1,2,0:T(2,128)} %param.11) | data formatting | bytes 512 | tf_op args[4]
  0.8 0.0 copy-start
  0.8 1.0 %copy-done = bf16[1,8,16,1536]{3,2,1,0:T(8,128)(2,1)S(1)} copy-done((bf16[1,8,16,1536]{3,2,1,0:T(8,128)(2,1)S(1)}, bf16[1,8,16,1536]{3,2,1,0:T(8,128)(2,1)}, u32[]{:S(2)}) %copy-start) | copy-done | bytes 393240
  1.8 0.0 copy-start.1
  1.8 1.0 %copy-done.1 = bf16[1,8,16,1536]{3,2,1,0:T(8,128)(2,1)S(1)} copy-done((bf16[1,8,16,1536]{3,2,1,0:T(8,128)(2,1)S(1)}, bf16[1,8,16,1536]{3,2,1,0:T(8,128)(2,1)}, u32[]{:S(2)}) %copy-start.1) | copy-done | bytes 393240
  2.8 0.0 copy-start.2
  2.8 1.0 %copy-done.2 = bf16[1,8,16,1536]{3,2,1,0:T(8,128)(2,1)S(1)} copy-done((bf16[1,8,16,1536]{3,2,1,0:T(8,128)(2,1)S(1)}, bf16[1,8,16,1536]{3,2,1,0:T(8,128)(2,1)}, u32[]{:S(2)}) %copy-start.2) | copy-done | bytes 393240
  3.8 0.0 copy-start.3
  3.8 0.7 %copy-done.3 = f32[3072]{0:T(1024)S(1)} copy-done((f32[3072]{0:T(1024)S(1)}, f32[3072]{0:T(1024)}, u32[]{:S(2)}) %copy-start.3) | copy-done | bytes 12312
  4.5 0.0 copy-start.4
  4.5 0.7 %copy-done.4 = s32[1,1,2,45]{3,2,1,0:T(2,128)S(1)} copy-done((s32[1,1,2,45]{3,2,1,0:T(2,128)S(1)}, s32[1,1,2,45]{3,2,1,0:T(2,128)}, u32[]{:S(2)}) %copy-start.4) | copy-done | bytes 384
  5.2 37.7 %shard_map.73 = bf16[128,3072]{1,0:T(8,128)(2,1)S(1)} custom-call(bf16[128,1536]{1,0:T(8,128)(2,1)S(1)} %bitcast.6, bf16[128,1536]{1,0:T(8,128)(2,1)S(1)} %bitcast.7, bf16[128,1536]{1,0:T(8,128)(2,1)S(1)} %bitcast.8, s32[1,1,2,45]{3,2,1,0:T(2,128)S(1)} %copy-done.4, s32[4,8,2]{2,1,0:T(8,128)S(1)} %copy.8.tv, bf16[1536,3072]{1,0:T(8,128)(2,1)} %w_hbm.1, ...), custom_call_target="tpu_custom_call" | custom-call | tf_op jit(solution)/shard_map/pallas_call | solution.py:397
  42.9 0.9 %copy.10 = bf16[1,8,16,3072]{3,2,1,0:T(8,128)(2,1)} copy(bf16[1,8,16,3072]{3,2,1,0:T(8,128)(2,1)S(1)} %bitcast.5) | data formatting | bytes 1572864
Async XLA Ops:
  0.8 1.0 %copy-start = (bf16[1,8,16,1536]{3,2,1,0:T(8,128)(2,1)S(1)}, bf16[1,8,16,1536]{3,2,1,0:T(8,128)(2,1)}, u32[]{:S(2)}) copy-start(bf16[1,8,16,1536]{3,2,1,0:T(8,128)(2,1)} %param.7) | copy-start | bytes 1179652
  1.8 1.0 %copy-start.1 = (bf16[1,8,16,1536]{3,2,1,0:T(8,128)(2,1)S(1)}, bf16[1,8,16,1536]{3,2,1,0:T(8,128)(2,1)}, u32[]{:S(2)}) copy-start(bf16[1,8,16,1536]{3,2,1,0:T(8,128)(2,1)} %param.8) | copy-start | bytes 1179652
  2.8 1.0 %copy-start.2 = (bf16[1,8,16,1536]{3,2,1,0:T(8,128)(2,1)S(1)}, bf16[1,8,16,1536]{3,2,1,0:T(8,128)(2,1)}, u32[]{:S(2)}) copy-start(bf16[1,8,16,1536]{3,2,1,0:T(8,128)(2,1)} %param.9) | copy-start | bytes 1179652
  3.8 0.7 %copy-start.3 = (f32[3072]{0:T(1024)S(1)}, f32[3072]{0:T(1024)}, u32[]{:S(2)}) copy-start(f32[3072]{0:T(1024)} %param.13) | copy-start | bytes 36868
  4.5 0.7 %copy-start.4 = (s32[1,1,2,45]{3,2,1,0:T(2,128)S(1)}, s32[1,1,2,45]{3,2,1,0:T(2,128)}, u32[]{:S(2)}) copy-start(s32[1,1,2,45]{3,2,1,0:T(2,128)} %wm.1) | copy-start | bytes 1084
